TPU v7x, 256 devices: a whole 4x4x8 slice. The times are simulated.
256 devices in a mesh: freq: 64 (over y_hi, z, x), pair: 4 (over y_lo, core).
Axes of the slice: x: 4, y: 4 (y_hi: 2, y_lo: 2; y = y_hi * 2 + y_lo), z: 8, core: 2. Of those that a mesh axis runs over, the one named last changes fastest.
Arguments:
- samples: bfloat16 [2048, 64, 2, 1024], P(('freq', 'pair')), may hold values from -6 to 6
- rfi_flags: int32 [64, 1024], P('freq'), may hold values 0 or 1
- feed_map: int32 [2048], replicated, may hold values from 0 to 2047, each once
Outputs:
- visibilities: bfloat16 [64, 2, 2048, 2048], P('freq', None, 'pair')
Inputs may be any that keep to these rules, and one draw needn't show every extreme that they name: `feed_map`: each of the 2048 feeds is assigned to exactly one slot.
All inputs are finite; a program needn't handle non-finite values. No bound on the sum of `rfi_flags` on one device may be relied on, other than what follows from the above.
Results may differ from a plain program's by a relative error of at most 0.001.
Values may be sent and summed in bfloat16 or wider, within the bound.
A program may use at most 64 MiB of HBM per device.

v0:
```python
import jax
import jax.numpy as jnp
from jax import lax
from jax.sharding import PartitionSpec as P


def local(samples, rfi_flags, feed_map):
    n_pair = lax.axis_size("pair")
    n_freq = lax.axis_size("freq")
    member = lax.axis_index("pair")
    keep_mask = (1 - rfi_flags).astype(jnp.bfloat16)
    shard_feeds = samples.shape[0]
    turned = lax.all_to_all(samples, "freq", split_axis=1, concat_axis=0, tiled=True)
    turned = turned * keep_mask[None, :, None, :]
    kept = lax.all_gather(turned, "pair", axis=0, tiled=True)
    shard_index = feed_map // shard_feeds
    within = feed_map % shard_feeds
    position = (
        shard_index % n_pair * (n_freq * shard_feeds) + shard_index // n_pair * shard_feeds + within
    )
    feed_count = kept.shape[0]
    steps_time = kept.shape[3]
    row_count = feed_count // n_pair
    inverse = 1.0 / steps_time
    feeds_all = kept[:, 0].reshape(feed_count, 2 * steps_time)
    columns = jnp.take(feeds_all, position, axis=0)
    own_rows = lax.dynamic_slice_in_dim(columns, member * row_count, row_count, 0)
    rotated_rows = jnp.concatenate([own_rows[:, steps_time:], -own_rows[:, :steps_time]], axis=1)
    stacked = jnp.concatenate([own_rows, rotated_rows], axis=0)
    product = lax.dot_general(
        stacked, columns, (((1,), (1,)), ((), ())), preferred_element_type=jnp.float32
    )
    results = [(product * inverse).astype(jnp.bfloat16).reshape(2, row_count, columns.shape[0])]
    computed = jnp.stack(results, axis=0)
    return computed


def solution(mesh):
    in_specs = (P(("freq", "pair"), None, None, None), P("freq", None), P())
    out_specs = P("freq", None, "pair", None)
    return jax.shard_map(local, mesh=mesh, in_specs=in_specs, out_specs=out_specs, check_vma=False)
```

profile of v0, /device:TPU:1, one launch (start us, length us, event | category | flops | bytes accessed | tf_op | source)
XLA Modules:
  0.0 236.9 jit_solution(12032836237903362301)
XLA Ops:
  6.5 0.0 copy-start.2
  6.5 0.0 copy-start.1
  6.5 5.2 %copy.6 = bf16[8,64,2,1024]{3,0,2,1:T(8,128)(2,1)} copy(bf16[8,64,2,1024]{3,2,1,0:T(2,128)(2,1)} %param.3) | data formatting | bytes 4194304 | tf_op args[0]
  11.7 15.1 %all-to-all-start = ((bf16[8,64,2,1024]{3,0,2,1:T(8,128)(2,1)}), bf16[8,64,2,1024]{3,0,2,1:T(8,128)(2,1)S(1)}, u32[]{:S(2)}, u32[]{:S(2)}) async-start(bf16[8,64,2,1024]{3,0,2,1:T(8,128)(2,1)} %copy.6), calls=%async_computation | async-start | bytes 4194304 | tf_op jit(solution)/shard_map/all_to_all | solution.py:13
  26.8 0.2 all-gather.2.cloned.1.call-start
  27.1 0.0 copy-done.2
  27.1 48.8 %all-to-all-done = bf16[8,64,2,1024]{3,0,2,1:T(8,128)(2,1)S(1)} async-done(((bf16[8,64,2,1024]{3,0,2,1:T(8,128)(2,1)}), bf16[8,64,2,1024]{3,0,2,1:T(8,128)(2,1)S(1)}, u32[]{:S(2)}, u32[]{:S(2)}) %all-to-all-start) | async-done | bytes 2097184 | tf_op jit(solution)/shard_map/all_to_all | solution.py:13
  75.9 1.5 bitcast_multiply_fusion
  77.3 0.0 all-gather.2.cloned.1.call-update
  77.4 0.0 copy-done.1
  77.4 82.8 %all-gather.2.cloned.1.call-done = bf16[2048,1,2,1024]{3,0,2,1:T(8,128)(2,1)} async-done(((bf16[512,1,2,1024]{3,0,2,1:T(8,128)(2,1)}), bf16[2048,1,2,1024]{3,0,2,1:T(8,128)(2,1)}) %all-gather.2.cloned.1.call-update) | async-done | bytes 8388624 | tf_op jit(solution)/shard_map/all_gather | solution.py:15
  160.2 16.4 %copy.8 = bf16[2048,1,2,1024]{3,2,0,1:T(2,128)(2,1)} copy(bf16[2048,1,2,1024]{3,0,2,1:T(8,128)(2,1)} %all-gather.2.cloned.1.call-done) | data formatting | bytes 16777216 | tf_op jit(solution)/shard_map/all_gather | solution.py:15
  176.6 10.1 %copy.9 = bf16[256,8,2,1024]{3,1,2,0:T(8,128)(2,1)} copy(bf16[256,8,2,1024]{3,2,1,0:T(2,128)(2,1)} %bitcast.13) | data formatting | bytes 16777216
  186.8 20.8 %gather_fusion = bf16[2048,2048]{1,0:T(8,128)(2,1)} fusion(bf16[2048,2048]{1,0:T(8,128)(2,1)} %bitcast.12, s32[2048]{0:T(1024)S(1)} %broadcast_clamp_fusion), kind=kCustom, calls=%fused_computation | custom fusion | bytes 16785408 | tf_op jit(solution)/shard_map/jit(_take)/gather | solution.py:26
  207.6 7.5 %broadcast_select_fusion = bf16[2048,2048]{1,0:T(8,128)(2,1)} fusion(bf16[2048,2048]{1,0:T(8,128)(2,1)} %gather_fusion, pred[2048]{0:T(1024)(128)(4,1)S(1)} %get-tuple-element.5), kind=kLoop, calls=%fused_computation.2 | loop fusion | flops 4194304 | bytes 16779264 | tf_op jit(solution)/shard_map/jit(_take)/select_n | solution.py:26
  215.0 0.0 copy-start
  215.0 1.9 constant_dynamic-slice_fusion
  216.9 2.2 fusion.16
  219.1 0.6 copy-done
  219.7 10.4 %multiply_convert_fusion = bf16[1024,2048]{1,0:T(8,128)(2,1)} fusion(bf16[2048,2048]{1,0:T(8,128)(2,1)S(1)} %copy-done, bf16[512,1024]{1,0:T(8,128)(2,1)S(1)} %get-tuple-element.8, bf16[512,1024]{1,0:T(8,128)(2,1)S(1)} %get-tuple-element.7, bf16[512,2048]{1,0:T(8,128)(2,1)S(1)} %constant_dynamic-slice_fusion), kind=kOutput, calls=%fused_computation.1 | convolution fusion | flops 8606711808 | bytes 16777216 | tf_op jit(solution)/shard_map/dot_general | solution.py:30
  (3 shorter events, 0.1 us)
Async XLA Ops:
  6.5 20.5 %copy-start.2 = (s32[1,1024]{1,0:T(1,128)S(1)}, s32[1,1024]{1,0:T(1,128)}, u32[]{:S(2)}) copy-start(s32[1,1024]{1,0:T(1,128)} %param.4) | copy-start | bytes 12292
  6.5 70.8 %copy-start.1 = (s32[2048]{0:T(1024)S(1)}, s32[2048]{0:T(1024)}, u32[]{:S(2)}) copy-start(s32[2048]{0:T(1024)} %param.5) | copy-start | bytes 24580
  11.7 64.2 %all-to-all-start = ((bf16[8,64,2,1024]{3,0,2,1:T(8,128)(2,1)}), bf16[8,64,2,1024]{3,0,2,1:T(8,128)(2,1)S(1)}, u32[]{:S(2)}, u32[]{:S(2)}) async-start(bf16[8,64,2,1024]{3,0,2,1:T(8,128)(2,1)} %copy.6), calls=%async_computation | async-start | bytes 4194304 | tf_op jit(solution)/shard_map/all_to_all | solution.py:13
  26.8 133.4 %all-gather.2.cloned.1.call-start = ((), (), s32[]{:S(2)}) async-start(), calls=%async_computation.1 | async-start | bytes 10485760 | tf_op jit(solution)/shard_map/all_gather | solution.py:15
  215.0 4.6 %copy-start = (bf16[2048,2048]{1,0:T(8,128)(2,1)S(1)}, bf16[2048,2048]{1,0:T(8,128)(2,1)}, u32[]{:S(2)}) copy-start(bf16[2048,2048]{1,0:T(8,128)(2,1)} %broadcast_select_fusion) | copy-start | bytes 25165828
Sparse Core Ops, SparseCore 0:
  77.5 82.6 all-gather.1
where the time goes:
time: 237 us
  waiting for transfers between devices  132 us (56%)
  local copies, waits for them, and re-layouts  55 us (23%)
  starting transfers between devices  15.3 us (6%)
  between operations  13.5 us (6%)
  other arithmetic  11.1 us (5%)
  matrix products  10.4 us (4%)
    all_gather x1, waiting for transfers between devices, local(): kept = lax.all_gather(turned, 'pair', axis=0, tiled=True)  82.8 us
    all_to_all x1, waiting for transfers between devices, local(): lax.all_to_all(samples, 'freq', split_axis=1, concat_axis=0, tiled=True)  48.8 us
    gather x1, local copies, waits for them, and re-layouts, local(): columns = jnp.take(feeds_all, position, axis=0)  20.8 us
    all_gather x1, local copies, waits for them, and re-layouts, local(): kept = lax.all_gather(turned, 'pair', axis=0, tiled=True)  16.4 us
    unnamed x8, local copies, waits for them, and re-layouts  15.9 us
    all_to_all x1, starting transfers between devices, local(): lax.all_to_all(samples, 'freq', split_axis=1, concat_axis=0, tiled=True)  15.1 us
    dot_general x1, matrix products, local(): lax.dot_general(stacked, columns, (((1,), (1,)), ((), ())), preferred_ele...  10.4 us
    select_n x1, other arithmetic, local(): columns = jnp.take(feeds_all, position, axis=0)  7.45 us
  transfers between devices with their start and end apart: 2, of which 2 were waited for; matrix products, arithmetic and copies ran while one was open for 0% of the time, Pallas kernels for 0%

commit v1 on v0

v1 whole, which is shorter than its diff:
```python
import jax
import jax.numpy as jnp
from jax import lax
from jax.experimental import pallas as pl
from jax.experimental.pallas import tpu as pltpu
from jax.sharding import PartitionSpec as P

MESH = pl.DeviceIdType.MESH
NC = 8
TC = 128
SLOTS = 2048
ROWS = 512


def kernel(samples, mask, slot_rows, out, zbuf, obuf, g, onehot, merged, ordered, left, acc, staged,
           zs, zr, xs, xr, own_s, own_r, out_s, out_r, fwd_s, fwd_r, core_s, core_r, write_s):
    fi = lax.axis_index("freq")
    member = lax.axis_index("pair")
    yh, z, x = fi // 32, (fi // 4) % 8, fi % 4
    yl, core = member // 2, member % 2
    y = yh * 2 + yl
    y_inner = yh * 2 + 1 - yl
    y_outer = 3 - y
    y_far = (1 - yh) * 2 + yl
    zpeers = [lax.rem(z + d, 8) for d in (4, 3, 5, 2, 6, 1, 7)]
    xpeers = [lax.rem(x + d, 4) for d in (2, 1, 3)]

    def device(yy, zz, xx, cc):
        return ((yy // 2 * 8 + zz) * 4 + xx, yy % 2 * 2 + cc)

    inner = device(y_inner, z, x, core)
    outer = device(y_outer, z, x, core)
    sibling = device(y, z, x, 1 - core)

    def remote(src, dst, send, recv, target):
        return pltpu.make_async_remote_copy(
            src_ref=src, dst_ref=dst, send_sem=send, recv_sem=recv, device_id=target, device_id_type=MESH
        )

    def wait(ref, sem):
        pltpu.make_async_copy(ref, ref, sem).wait()

    barrier = pltpu.get_barrier_semaphore()
    targets = [device(y, zz, x, core) for zz in zpeers] + [device(y, z, xx, core) for xx in xpeers]
    targets += [inner, outer, sibling]
    for target in targets:
        pl.semaphore_signal(barrier, inc=1, device_id=target, device_id_type=MESH)
    pl.semaphore_wait(barrier, len(targets))

    def z_send(j):
        k, h = j // 2, j % 2
        half = jnp.where(h == 0, 1 - yh, yh)
        pltpu.make_async_copy(samples.at[k, half, z], zbuf.at[j, z], zr.at[j]).start()
        for zz in zpeers:
            remote(samples.at[k, half, zz], zbuf.at[j, z], zs.at[j], zr.at[j], device(y, zz, x, core)).start()

    def x_send(k, h):
        j = 2 * k + h
        wait(zbuf.at[j], zr.at[j])
        dst = g.at[k, core, y, x] if h else obuf.at[k, x]
        pltpu.make_async_copy(zbuf.at[j, :, x], dst, xr.at[j]).start()
        for xx in xpeers:
            remote(zbuf.at[j, :, xx], dst, xs.at[j], xr.at[j], device(y, z, xx, core)).start()

    def core_send(k, yy):
        remote(g.at[k, core, yy], g.at[k, core, yy], core_s.at[k], core_r.at[k], sibling).start()

    def y_send(k, h):
        j = 2 * k + h
        if h:
            wait(g.at[k, core, y], xr.at[j])
            remote(g.at[k, core, y], g.at[k, core, y], own_s.at[k], own_r.at[k], inner).start()
            core_send(k, y)
        else:
            wait(obuf.at[k], xr.at[j])
            remote(obuf.at[k], g.at[k, core, y], out_s.at[k], out_r.at[k], outer).start()

    def forward(k):
        block = g.at[k, core, y_outer]
        wait(block, out_r.at[k])
        remote(block, block, fwd_s.at[k], fwd_r.at[k], inner).start()
        core_send(k, y_outer)

    def own_arrived(k):
        wait(g.at[k, core, y_inner], own_r.at[k])
        core_send(k, y_inner)

    def forward_arrived(k):
        wait(g.at[k, core, y_far], fwd_r.at[k])
        core_send(k, y_far)

    def permute(k, block):
        @pl.loop(0, 2)
        def _(i):
            rows = pl.ds(pl.multiple_of(block * 1024 + i * 512, 512), 512)
            ordered[rows, :] = jnp.dot(
                onehot[rows, :], merged[...], preferred_element_type=jnp.float32
            ).astype(jnp.bfloat16)

    def start_compute(k):
        wait(g.at[k, 1 - core], core_r.at[k])
        keep = mask[k]

        @pl.loop(0, 8)
        def _(b):
            rows = pl.ds(pl.multiple_of(b * 256, 256), 256)
            block = g[k, b // 4, b % 4].reshape(32, 16, TC) * keep
            merged[rows, :TC] = block[:, :8].reshape(256, TC)
            merged[rows, TC:] = block[:, 8:].reshape(256, TC)

        permute(k, 0)

    def prepare_left():
        own = ordered[pl.ds(pl.multiple_of(member * ROWS, ROWS), ROWS), :]
        left[:ROWS, :] = own
        left[ROWS:, :TC] = own[:, TC:]
        left[ROWS:, TC:] = -own[:, :TC]

    def product(k, half):
        @pl.when(k < NC - 1)
        def _():
            @pl.loop(0, 2)
            def _(i):
                n = half * 2 + i
                rows = pl.ds(pl.multiple_of(n * 512, 512), 512)
                acc[n] += lax.dot_general(
                    left[...], ordered[rows, :], (((1,), (1,)), ((), ())), preferred_element_type=jnp.float32
                )

        @pl.when(k == NC - 1)
        def _():
            @pl.loop(0, 2)
            def _(i):
                n = half * 2 + i
                rows = pl.ds(pl.multiple_of(n * 512, 512), 512)
                total = acc[n] + lax.dot_general(
                    left[...], ordered[rows, :], (((1,), (1,)), ((), ())), preferred_element_type=jnp.float32
                )
                staged[n] = (total * (1.0 / (NC * TC))).astype(jnp.bfloat16).reshape(2, ROWS, 512)
                pltpu.make_async_copy(staged.at[n], out.at[0, :, :, rows], write_s.at[n]).start()

    for j in range(4):
        z_send(j)

    @pl.loop(0, 16)
    def _(b):
        rows = pl.ds(pl.multiple_of(b * 128, 128), 128)
        spot = slot_rows[rows, :]
        hit = spot == lax.broadcasted_iota(jnp.int32, (128, SLOTS), 1)
        onehot[rows, :] = jnp.where(hit, 1.0, 0.0).astype(jnp.bfloat16)

    @pl.loop(0, 4)
    def _(n):
        acc[n] = jnp.zeros((2 * ROWS, 512), jnp.float32)

    def step(s, carry):
        @pl.when(s < NC)
        def _():
            x_send(s, 0)

        @pl.when(s + 2 < NC)
        def _():
            z_send(2 * s + 4)

        @pl.when(s >= 2)
        def _():
            start_compute(s - 2)

        @pl.when((s >= 1) & (s < NC + 1))
        def _():
            own_arrived(s - 1)

        @pl.when(s < NC)
        def _():
            y_send(s, 0)

        @pl.when(s >= 2)
        def _():
            permute(s - 2, 1)

        @pl.when(s < NC)
        def _():
            x_send(s, 1)

        @pl.when(s + 2 < NC)
        def _():
            z_send(2 * s + 5)

        @pl.when(s >= 2)
        def _():
            prepare_left()
            product(s - 2, 0)

        @pl.when(s < NC)
        def _():
            y_send(s, 1)
            forward(s)

        @pl.when((s >= 1) & (s < NC + 1))
        def _():
            forward_arrived(s - 1)

        @pl.when(s >= 2)
        def _():
            product(s - 2, 1)

        return carry

    lax.fori_loop(0, NC + 2, step, 0)

    @pl.loop(0, NC)
    def _(k):
        for h in range(2):
            wait(zbuf.at[2 * k + h, pl.ds(0, 7)], zs.at[2 * k + h])
            wait(obuf.at[k, pl.ds(0, 3)], xs.at[2 * k + h])
        wait(obuf.at[k], own_s.at[k])
        wait(obuf.at[k], out_s.at[k])
        wait(obuf.at[k], fwd_s.at[k])
        wait(g.at[k, 0], core_s.at[k])

    @pl.loop(0, 4)
    def _(n):
        rows = pl.ds(pl.multiple_of(n * 512, 512), 512)
        pltpu.make_async_copy(staged.at[n], out.at[0, :, :, rows], write_s.at[n]).wait()


def local(samples, rfi_flags, feed_map):
    feeds = samples.shape[0]
    turned = samples.reshape(feeds, 2, 8, 4, 2, NC, TC).transpose(5, 1, 2, 3, 4, 0, 6)
    turned = turned.reshape(NC, 2, 8, 4, 2 * feeds, TC)
    mask = (1 - rfi_flags).astype(jnp.bfloat16).reshape(NC, 1, TC)
    mask = jnp.broadcast_to(mask, (NC, 2 * feeds, TC))
    w, shard = feed_map % 8, feed_map // 8
    core, yl, x, z, yh = shard % 2, shard // 2 % 2, shard // 4 % 4, shard // 16 % 8, shard // 128
    spot = (((core * 4 + yh * 2 + yl) * 4 + x) * 8 + z) * 8 + w
    dma = pltpu.SemaphoreType.DMA
    vmem = pl.BlockSpec(memory_space=pltpu.VMEM)
    return pl.pallas_call(
        kernel,
        out_shape=jax.ShapeDtypeStruct((1, 2, ROWS, SLOTS), jnp.bfloat16),
        in_specs=[pl.BlockSpec(memory_space=pl.ANY), vmem, vmem],
        out_specs=pl.BlockSpec(memory_space=pl.ANY),
        scratch_shapes=[
            pltpu.VMEM((2 * NC, 8, 4, 16, TC), jnp.bfloat16),
            pltpu.VMEM((NC, 4, 8, 16, TC), jnp.bfloat16),
            pltpu.VMEM((NC, 2, 4, 4, 8, 16, TC), jnp.bfloat16),
            pltpu.VMEM((SLOTS, SLOTS), jnp.bfloat16),
            pltpu.VMEM((SLOTS, 2 * TC), jnp.bfloat16),
            pltpu.VMEM((SLOTS, 2 * TC), jnp.bfloat16),
            pltpu.VMEM((2 * ROWS, 2 * TC), jnp.bfloat16),
            pltpu.VMEM((4, 2 * ROWS, 512), jnp.float32),
            pltpu.VMEM((4, 2, ROWS, 512), jnp.bfloat16),
            dma((2 * NC,)), dma((2 * NC,)), dma((2 * NC,)), dma((2 * NC,)),
            dma((NC,)), dma((NC,)), dma((NC,)), dma((NC,)), dma((NC,)), dma((NC,)), dma((NC,)), dma((NC,)),
            dma((4,)),
        ],
        compiler_params=pltpu.CompilerParams(
            collective_id=0, has_side_effects=True, vmem_limit_bytes=56 * 1024 * 1024
        ),
        cost_estimate=pl.CostEstimate(flops=26 * 10**9, bytes_accessed=6 * 2**20, transcendentals=0),
        name="correlate",
    )(turned, mask, spot.reshape(SLOTS, 1))


def solution(mesh):
    in_specs = (P(("freq", "pair"), None, None, None), P("freq", None), P())
    out_specs = P("freq", None, "pair", None)
    return jax.shard_map(local, mesh=mesh, in_specs=in_specs, out_specs=out_specs, check_vma=False)
```

time: 237 us -> 123 us (0.52)
  waiting for transfers between devices: 132 us -> 0 us
  Pallas kernels: 0 us -> 109 us
  local copies, waits for them, and re-layouts: 55 us -> 12.6 us
  starting transfers between devices: 15.3 us -> 0 us
  between operations: 13.5 us -> 0.02 us
  matrix products: 10.4 us -> 0 us
  other arithmetic: 11.1 us -> 1.45 us
    pallas_call x0 -> x1, Pallas kernels: none -> 109 us  [local(): pl.pallas_call(kernel, out_shape=jax.ShapeDtypeStruct((1, 2, ROWS, SLOTS)...]
    all_gather x1 -> x0, waiting for transfers between devices: 82.8 us -> none  [local(): kept = lax.all_gather(turned, 'pair', axis=0, tiled=True)]
    all_to_all x1 -> x0, waiting for transfers between devices: 48.8 us -> none  [local(): lax.all_to_all(samples, 'freq', split_axis=1, concat_axis=0, tiled=True)]
    gather x1 -> x0, local copies, waits for them, and re-layouts: 20.8 us -> none  [local(): columns = jnp.take(feeds_all, position, axis=0)]
    all_gather x1 -> x0, local copies, waits for them, and re-layouts: 16.4 us -> none  [local(): kept = lax.all_gather(turned, 'pair', axis=0, tiled=True)]
    all_to_all x1 -> x0, starting transfers between devices: 15.1 us -> none  [local(): lax.all_to_all(samples, 'freq', split_axis=1, concat_axis=0, tiled=True)]
    unnamed x8 -> x1, local copies, waits for them, and re-layouts: 15.9 us -> 4.79 us
    dot_general x1 -> x0, matrix products: 10.4 us -> none  [local(): lax.dot_general(stacked, columns, (((1,), (1,)), ((), ())), preferred_ele...]
  transfers between devices with their start and end apart: 2 -> 0, of which waited for: 2 -> 0; matrix products, arithmetic and copies ran while one was open for 0% -> 0% of each run, Pallas kernels for 0% -> 0%
where the time goes in v1:
time: 123 us
  Pallas kernels  109 us (89%)
  local copies, waits for them, and re-layouts  12.6 us (10%)
  other arithmetic  1.45 us (1%)
    pallas_call x1, Pallas kernels, local(): pl.pallas_call(kernel, out_shape=jax.ShapeDtypeStruct((1, 2, ROWS, SLOTS)...  109 us
    reshape x2, local copies, waits for them, and re-layouts, local(): samples.reshape(feeds, 2, 8, 4, 2, NC, TC).transpose(5, 1, 2, 3, 4, 0, 6)  5.82 us
    unnamed x1, local copies, waits for them, and re-layouts  4.79 us

profile of v1, /device:TPU:1, one launch (start us, length us, event | category | flops | bytes accessed | tf_op | source)
XLA Modules:
  0.0 123.2 jit_solution(10921921903765752008)
XLA Ops:
  0.0 0.7 convert_reduce_fusion
  0.7 0.7 fusion.8
  1.5 0.6 broadcast_in_dim.8.mask
  2.1 1.4 %copy.6.slot_rows = s32[2048,1]{1,0:T(8,128)} copy(s32[2048,1]{0,1:T(1,128)S(1)} %bitcast.8) | data formatting | bytes 16384 | tf_op jit(solution)/shard_map/reshape | solution.py:262
  3.4 3.2 %reshape.11 = bf16[8,2,8,4,2,8,128]{6,5,4,3,2,1,0:T(8,128)(2,1)S(1)} reshape(bf16[8,64,2,1024]{3,2,1,0:T(2,128)(2,1)} %param.3) | data formatting | bytes 4194304 | tf_op jit(solution)/shard_map/reshape | solution.py:229
  6.6 2.7 %copy.8 = bf16[8,2,8,4,2,8,128]{6,0,4,3,2,1,5:T(8,128)(2,1)} copy(bf16[8,2,8,4,2,8,128]{6,5,4,3,2,1,0:T(8,128)(2,1)S(1)} %reshape.11) | data formatting | bytes 4194304 | tf_op jit(solution)/shard_map/reshape | solution.py:229
  9.2 109.2 %correlate.1 = bf16[1,2,512,2048]{3,2,1,0:T(8,128)(2,1)} custom-call(bf16[8,2,8,4,16,128]{5,4,3,2,1,0:T(8,128)(2,1)} %bitcast.7, bf16[8,16,128]{2,1,0:T(8,128)(2,1)} %broadcast_in_dim.8.mask, s32[2048,1]{1,0:T(8,128)} %copy.6.slot_rows), custom_call_target="tpu_custom_call" | custom-call | flops 25999998976 | bytes 6291456 | tf_op jit(solution)/shard_map/correlate/pallas_call | solution.py:238
  118.4 4.8 %copy.10 = bf16[1,2,512,2048]{3,2,1,0:T(8,128)(2,1)} copy(bf16[1,2,512,2048]{3,2,1,0:T(8,128)(2,1)} %correlate.1) | data formatting | bytes 8388608

commit v2 on v1

v2 whole, which is shorter than its diff:
```python
import jax
import jax.numpy as jnp
from jax import lax
from jax.experimental import pallas as pl
from jax.experimental.pallas import tpu as pltpu
from jax.sharding import PartitionSpec as P

MESH = pl.DeviceIdType.MESH
NC = 8
TC = 128
SLOTS = 2048
ROWS = 512


def kernel(raw_samples, flags, feeds, out, raw, samples, zbuf, obuf, g, onehot, merged, ordered, left, acc, staged,
           zs, zr, xs, xr, own_s, own_r, out_s, out_r, fwd_s, fwd_r, core_s, core_r, pair_s, pair_r, write_s, raw_s):
    fi = lax.axis_index("freq")
    member = lax.axis_index("pair")
    yh, z, x = fi // 32, (fi // 4) % 8, fi % 4
    yl, core = member // 2, member % 2
    y = yh * 2 + yl
    y_inner = yh * 2 + 1 - yl
    y_outer = 3 - y
    y_far = (1 - yh) * 2 + yl
    zpeers = [lax.rem(z + d, 8) for d in (4, 3, 5, 2, 6, 1, 7)]
    xpeers = [lax.rem(x + d, 4) for d in (2, 1, 3)]

    def device(yy, zz, xx, cc):
        return ((yy // 2 * 8 + zz) * 4 + xx, yy % 2 * 2 + cc)

    inner = device(y_inner, z, x, core)
    outer = device(y_outer, z, x, core)
    sibling = device(y, z, x, 1 - core)

    def remote(src, dst, send, recv, target):
        return pltpu.make_async_remote_copy(
            src_ref=src, dst_ref=dst, send_sem=send, recv_sem=recv, device_id=target, device_id_type=MESH
        )

    def wait(ref, sem):
        pltpu.make_async_copy(ref, ref, sem).wait()

    load = pltpu.make_async_copy(raw_samples, raw, raw_s)
    load.start()
    barrier = pltpu.get_barrier_semaphore()
    targets = [device(y, zz, x, core) for zz in zpeers] + [device(y, z, xx, core) for xx in xpeers]
    targets += [inner, outer, sibling]
    for target in targets:
        pl.semaphore_signal(barrier, inc=1, device_id=target, device_id_type=MESH)

    def pack(k):
        times = pl.ds(pl.multiple_of(k * TC, TC), TC)

        @pl.loop(0, 8)
        def _(b):
            block = raw[:, pl.ds(pl.multiple_of(b * 8, 8), 8), :, times]
            packed = jnp.transpose(block, (1, 2, 0, 3)).reshape(2, 4, 16, TC)
            samples[k, b // 4, pl.ds(pl.multiple_of(b % 4 * 2, 2), 2)] = packed


    def z_send(j):
        k, h = j // 2, j % 2
        half = jnp.where(h == 0, 1 - yh, yh)
        pltpu.make_async_copy(samples.at[k, half, z], zbuf.at[j, z], zr.at[j]).start()
        for zz in zpeers:
            remote(samples.at[k, half, zz], zbuf.at[j, z], zs.at[j], zr.at[j], device(y, zz, x, core)).start()

    def x_send(k, h):
        j = 2 * k + h
        wait(zbuf.at[j], zr.at[j])
        dst = g.at[k, core, y, x] if h else obuf.at[k, x]
        pltpu.make_async_copy(zbuf.at[j, :, x], dst, xr.at[j]).start()
        for xx in xpeers:
            remote(zbuf.at[j, :, xx], dst, xs.at[j], xr.at[j], device(y, z, xx, core)).start()

    def core_send(k, yy):
        remote(g.at[k, core, yy], g.at[k, core, yy], core_s.at[k], core_r.at[k], sibling).start()

    def y_send(k, h):
        j = 2 * k + h
        if h:
            wait(g.at[k, core, y], xr.at[j])
            remote(g.at[k, core, y], g.at[k, core, y], own_s.at[k], own_r.at[k], inner).start()
            core_send(k, y)
        else:
            wait(obuf.at[k], xr.at[j])
            remote(obuf.at[k], g.at[k, core, y], out_s.at[k], out_r.at[k], outer).start()

    def forward(k):
        block = g.at[k, core, y_outer]
        wait(block, out_r.at[k])
        remote(block, block, fwd_s.at[k], fwd_r.at[k], inner).start()
        core_send(k, y_outer)

    def own_arrived(k):
        wait(g.at[k, core, y_inner], own_r.at[k])
        core_send(k, y_inner)

    def forward_arrived(k):
        wait(g.at[k, core, y_far], fwd_r.at[k])
        core_send(k, y_far)

    def order(k):
        wait(g.at[k, 1 - core], core_r.at[k])
        times = pl.ds(pl.multiple_of(k * TC, TC), TC)
        keep = jnp.broadcast_to((1 - flags[:, times]).astype(jnp.float32), (16, TC)).astype(jnp.bfloat16)

        @pl.loop(0, 8)
        def _(b):
            rows = pl.ds(pl.multiple_of(b * 256, 256), 256)
            block = g[k, b // 4, b % 4].reshape(32, 16, TC) * keep
            merged[rows, :TC] = block[:, :8].reshape(256, TC)
            merged[rows, TC:] = block[:, 8:].reshape(256, TC)

        picked = jnp.dot(onehot[...], merged[...], preferred_element_type=jnp.float32).astype(jnp.bfloat16)
        ordered[k, :, core] = picked.reshape(2, ROWS, 2 * TC)
        pair_copy(k).start()

    def pair_copy(k):
        block = ordered.at[k, :, core]
        return remote(block, block, pair_s.at[k], pair_r.at[k], sibling)

    def prepare_left(k):
        own = ordered[k, yl, core]
        left[:ROWS, :] = own
        left[ROWS:, :TC] = own[:, TC:]
        left[ROWS:, TC:] = -own[:, :TC]

    def multiply(k, half):
        return lax.dot_general(
            left[...],
            ordered[k, :, half].reshape(2 * ROWS, 2 * TC),
            (((1,), (1,)), ((), ())),
            preferred_element_type=jnp.float32,
        )

    def write(half, i):
        columns = pl.ds(pl.multiple_of((i * 2 + half) * ROWS, ROWS), ROWS)
        return pltpu.make_async_copy(staged.at[half, i], out.at[0, :, :, columns], write_s.at[half, i])

    def product(k, half):
        @pl.when(k < NC - 1)
        def _():
            acc[half] += multiply(k, half)

        @pl.when(k == NC - 1)
        def _():
            total = (acc[half] + multiply(k, half)) * (1.0 / (NC * TC))
            for i in range(2):
                staged[half, i] = total[:, i * ROWS : (i + 1) * ROWS].astype(jnp.bfloat16).reshape(2, ROWS, ROWS)
                write(half, i).start()

    load.wait()
    pack(0)
    pl.semaphore_wait(barrier, len(targets))
    z_send(0)
    z_send(1)
    pack(1)
    z_send(2)
    z_send(3)

    @pl.loop(0, 8)
    def _(b):
        feed = feeds[pl.ds((b // 4 * 2 + core) * 4 + b % 4, 1), :]
        w, c, l = feed & 7, (feed >> 3) & 1, (feed >> 4) & 1
        xx, zz, h = (feed >> 5) & 3, (feed >> 7) & 7, feed >> 10
        spot = ((((c * 4 + h * 2 + l) * 4 + xx) * 8 + zz) * 8 + w).astype(jnp.float32)
        spot = jnp.broadcast_to(spot, (128, 128)).T.astype(jnp.int32)
        for n in range(SLOTS // 128):
            hit = spot == lax.broadcasted_iota(jnp.int32, (128, 128), 1) + n * 128
            onehot[pl.ds(pl.multiple_of(b * 128, 128), 128), n * 128 : (n + 1) * 128] = jnp.where(
                hit, 1.0, 0.0
            ).astype(jnp.bfloat16)

    for half in range(2):
        acc[half] = jnp.zeros((2 * ROWS, 2 * ROWS), jnp.float32)

    def step(s, carry):
        @pl.when(s < NC)
        def _():
            x_send(s, 0)

        @pl.when(s + 2 < NC)
        def _():
            pack(s + 2)
            z_send(2 * s + 4)

        @pl.when((s >= 1) & (s < NC + 1))
        def _():
            y_send((s - 1), 0)

        @pl.when((s >= 1) & (s < NC + 1))
        def _():
            y_send((s - 1), 1)

        @pl.when((s >= 2) & (s < NC + 2))
        def _():
            forward((s - 2))

        @pl.when(s >= 4)
        def _():
            order((s - 4))

        @pl.when(s < NC)
        def _():
            x_send(s, 1)

        @pl.when(s + 2 < NC)
        def _():
            z_send(2 * s + 5)

        @pl.when(s >= 4)
        def _():
            prepare_left((s - 4))
            product((s - 4), core)

        @pl.when((s >= 2) & (s < NC + 2))
        def _():
            own_arrived((s - 2))

        @pl.when(s >= 4)
        def _():
            wait(ordered.at[(s - 4), :, 1 - core], pair_r.at[(s - 4)])
            product((s - 4), 1 - core)

        @pl.when((s >= 3) & (s < NC + 3))
        def _():
            forward_arrived((s - 3))

        return carry

    lax.fori_loop(0, NC + 4, step, 0)

    @pl.loop(0, NC)
    def _(k):
        for h in range(2):
            wait(zbuf.at[2 * k + h, pl.ds(0, 7)], zs.at[2 * k + h])
            wait(obuf.at[k, pl.ds(0, 3)], xs.at[2 * k + h])
        wait(obuf.at[k], own_s.at[k])
        wait(obuf.at[k], out_s.at[k])
        wait(obuf.at[k], fwd_s.at[k])
        wait(g.at[k, 0], core_s.at[k])
        wait(ordered.at[k, :, core], pair_s.at[k])

    for half in range(2):
        for i in range(2):
            write(half, i).wait()


def local(samples, rfi_flags, feed_map):
    dma = pltpu.SemaphoreType.DMA
    vmem = pl.BlockSpec(memory_space=pltpu.VMEM)
    return pl.pallas_call(
        kernel,
        out_shape=jax.ShapeDtypeStruct((1, 2, ROWS, SLOTS), jnp.bfloat16),
        in_specs=[pl.BlockSpec(memory_space=pltpu.HBM), vmem, vmem],
        out_specs=pl.BlockSpec(memory_space=pl.ANY),
        scratch_shapes=[
            pltpu.VMEM((8, 64, 2, NC * TC), jnp.bfloat16),
            pltpu.VMEM((NC, 2, 8, 4, 16, TC), jnp.bfloat16),
            pltpu.VMEM((2 * NC, 8, 4, 16, TC), jnp.bfloat16),
            pltpu.VMEM((NC, 4, 8, 16, TC), jnp.bfloat16),
            pltpu.VMEM((NC, 2, 4, 4, 8, 16, TC), jnp.bfloat16),
            pltpu.VMEM((2 * ROWS, SLOTS), jnp.bfloat16),
            pltpu.VMEM((SLOTS, 2 * TC), jnp.bfloat16),
            pltpu.VMEM((NC, 2, 2, ROWS, 2 * TC), jnp.bfloat16),
            pltpu.VMEM((2 * ROWS, 2 * TC), jnp.bfloat16),
            pltpu.VMEM((2, 2 * ROWS, 2 * ROWS), jnp.float32),
            pltpu.VMEM((2, 2, 2, ROWS, ROWS), jnp.bfloat16),
            dma((2 * NC,)), dma((2 * NC,)), dma((2 * NC,)), dma((2 * NC,)),
            dma((NC,)), dma((NC,)), dma((NC,)), dma((NC,)), dma((NC,)), dma((NC,)), dma((NC,)), dma((NC,)),
            dma((NC,)), dma((NC,)), dma((2, 2)), dma,
        ],
        compiler_params=pltpu.CompilerParams(
            collective_id=0, has_side_effects=True, vmem_limit_bytes=46 * 1024 * 1024
        ),
        cost_estimate=pl.CostEstimate(flops=26 * 10**9, bytes_accessed=6 * 2**20, transcendentals=0),
        name="correlate",
    )(samples, rfi_flags, feed_map.reshape(16, 128))


def solution(mesh):
    in_specs = (P(("freq", "pair"), None, None, None), P("freq", None), P())
    out_specs = P("freq", None, "pair", None)
    return jax.shard_map(local, mesh=mesh, in_specs=in_specs, out_specs=out_specs, check_vma=False)
```

time: 123 us -> 87.7 us (0.71)
  Pallas kernels: 109 us -> 82.5 us
  local copies, waits for them, and re-layouts: 12.6 us -> 4.99 us
  other arithmetic: 1.45 us -> 0 us
    pallas_call x1, Pallas kernels: 109 us -> 82.5 us  [local(): pl.pallas_call(kernel, out_shape=jax.ShapeDtypeStruct((1, 2, ROWS, SLOTS)...]
    reshape x3 -> x0, local copies, waits for them, and re-layouts: 7.17 us -> none  [the longest x2 5.82 us: local(): samples.reshape(feeds, 2, 8, 4, 2, NC, TC).transpose(5, 1, 2, 3, 4, 0, 6)]
    unnamed x1 -> x7, local copies, waits for them, and re-layouts: 4.79 us -> 4.99 us
where the time goes in v2:
time: 87.7 us; the launch traced here: 87.5 us
  Pallas kernels  82.5 us (94%)
  local copies, waits for them, and re-layouts  4.99 us (6%)
    pallas_call x1, Pallas kernels, local(): pl.pallas_call(kernel, out_shape=jax.ShapeDtypeStruct((1, 2, ROWS, SLOTS)...  82.5 us
    unnamed x7, local copies, waits for them, and re-layouts  4.99 us

profile of v2, /device:TPU:1, one launch (start us, length us, event | category | flops | bytes accessed | tf_op | source)
XLA Modules:
  0.0 87.5 jit_solution(6458216572341537161)
XLA Ops:
  0.0 0.0 copy-start
  0.0 1.6 %copy-done = bf16[8,64,2,1024]{3,2,1,0:T(2,128)(2,1)S(1)} copy-done((bf16[8,64,2,1024]{3,2,1,0:T(2,128)(2,1)S(1)}, bf16[8,64,2,1024]{3,2,1,0:T(2,128)(2,1)}, u32[]{:S(2)}) %copy-start) | copy-done | bytes 2097176
  1.6 0.0 copy-start.1
  1.6 0.7 copy-done.1
  2.3 0.0 copy-start.2
  2.3 0.7 copy-done.2
  3.0 82.5 %correlate.1 = bf16[1,2,512,2048]{3,2,1,0:T(8,128)(2,1)S(1)} custom-call(bf16[8,64,2,1024]{3,2,1,0:T(2,128)(2,1)S(1)} %copy-done, s32[1,1024]{1,0:T(1,128)S(1)} %copy-done.2, s32[16,128]{1,0:T(8,128)S(1)} %bitcast.1), custom_call_target="tpu_custom_call" | custom-call | flops 25999998976 | bytes 6291456 | tf_op jit(solution)/shard_map/correlate/pallas_call | solution.py:253
  85.5 2.0 %copy.5 = bf16[1,2,512,2048]{3,2,1,0:T(8,128)(2,1)} copy(bf16[1,2,512,2048]{3,2,1,0:T(8,128)(2,1)S(1)} %correlate.1) | data formatting | bytes 8388608
Async XLA Ops:
  0.0 1.6 %copy-start = (bf16[8,64,2,1024]{3,2,1,0:T(2,128)(2,1)S(1)}, bf16[8,64,2,1024]{3,2,1,0:T(2,128)(2,1)}, u32[]{:S(2)}) copy-start(bf16[8,64,2,1024]{3,2,1,0:T(2,128)(2,1)} %raw_samples.1) | copy-start | bytes 6291460
  1.6 0.7 copy-start.1
  2.3 0.7 copy-start.2

commit v3 on v2

--- a/solution.py
+++ b/solution.py
@@ -12,8 +12,8 @@
 ROWS = 512
 
 
-def kernel(raw_samples, flags, feeds, out, raw, samples, zbuf, obuf, g, onehot, merged, ordered, left, acc, staged,
-           zs, zr, xs, xr, own_s, own_r, out_s, out_r, fwd_s, fwd_r, core_s, core_r, pair_s, pair_r, write_s, raw_s):
+def kernel(raw, flags, feeds, out, samples, zbuf, obuf, g, onehot, merged, ordered, left, acc, staged,
+           zs, zr, xs, xr, own_s, own_r, out_s, out_r, fwd_s, fwd_r, core_s, core_r, pair_s, pair_r, write_s):
     fi = lax.axis_index("freq")
     member = lax.axis_index("pair")
     yh, z, x = fi // 32, (fi // 4) % 8, fi % 4
@@ -40,8 +40,6 @@
     def wait(ref, sem):
         pltpu.make_async_copy(ref, ref, sem).wait()
 
-    load = pltpu.make_async_copy(raw_samples, raw, raw_s)
-    load.start()
     barrier = pltpu.get_barrier_semaphore()
     targets = [device(y, zz, x, core) for zz in zpeers] + [device(y, z, xx, core) for xx in xpeers]
     targets += [inner, outer, sibling]
@@ -150,7 +148,6 @@
                 staged[half, i] = total[:, i * ROWS : (i + 1) * ROWS].astype(jnp.bfloat16).reshape(2, ROWS, ROWS)
                 write(half, i).start()
 
-    load.wait()
     pack(0)
     pl.semaphore_wait(barrier, len(targets))
     z_send(0)
@@ -189,25 +186,25 @@
         def _():
             y_send((s - 1), 0)
 
+        @pl.when(s < NC)
+        def _():
+            x_send(s, 1)
+
+        @pl.when(s + 2 < NC)
+        def _():
+            z_send(2 * s + 5)
+
         @pl.when((s >= 1) & (s < NC + 1))
         def _():
             y_send((s - 1), 1)
 
+        @pl.when(s >= 4)
+        def _():
+            order((s - 4))
+
         @pl.when((s >= 2) & (s < NC + 2))
         def _():
             forward((s - 2))
-
-        @pl.when(s >= 4)
-        def _():
-            order((s - 4))
-
-        @pl.when(s < NC)
-        def _():
-            x_send(s, 1)
-
-        @pl.when(s + 2 < NC)
-        def _():
-            z_send(2 * s + 5)
 
         @pl.when(s >= 4)
         def _():
@@ -253,10 +250,9 @@
     return pl.pallas_call(
         kernel,
         out_shape=jax.ShapeDtypeStruct((1, 2, ROWS, SLOTS), jnp.bfloat16),
-        in_specs=[pl.BlockSpec(memory_space=pltpu.HBM), vmem, vmem],
+        in_specs=[vmem, vmem, vmem],
         out_specs=pl.BlockSpec(memory_space=pl.ANY),
         scratch_shapes=[
-            pltpu.VMEM((8, 64, 2, NC * TC), jnp.bfloat16),
             pltpu.VMEM((NC, 2, 8, 4, 16, TC), jnp.bfloat16),
             pltpu.VMEM((2 * NC, 8, 4, 16, TC), jnp.bfloat16),
             pltpu.VMEM((NC, 4, 8, 16, TC), jnp.bfloat16),
@@ -269,7 +265,7 @@
             pltpu.VMEM((2, 2, 2, ROWS, ROWS), jnp.bfloat16),
             dma((2 * NC,)), dma((2 * NC,)), dma((2 * NC,)), dma((2 * NC,)),
             dma((NC,)), dma((NC,)), dma((NC,)), dma((NC,)), dma((NC,)), dma((NC,)), dma((NC,)), dma((NC,)),
-            dma((NC,)), dma((NC,)), dma((2, 2)), dma,
+            dma((NC,)), dma((NC,)), dma((2, 2)),
         ],
         compiler_params=pltpu.CompilerParams(
             collective_id=0, has_side_effects=True, vmem_limit_bytes=46 * 1024 * 1024

time: 87.7 us -> 87.4 us (level)
  no operation moved by 1% of the time
where the time goes in v3:
time: 87.4 us; the launch traced here: 87.2 us
  Pallas kernels  82.2 us (94%)
  local copies, waits for them, and re-layouts  4.99 us (6%)
    pallas_call x1, Pallas kernels, local(): pl.pallas_call(kernel, out_shape=jax.ShapeDtypeStruct((1, 2, ROWS, SLOTS)...  82.2 us
    unnamed x7, local copies, waits for them, and re-layouts  4.99 us

profile of v3, /device:TPU:1, one launch (start us, length us, event | category | flops | bytes accessed | tf_op | source)
XLA Modules:
  0.0 87.2 jit_solution(13073671439146621662)
XLA Ops:
  0.0 0.0 copy-start
  0.0 1.6 %copy-done = bf16[8,64,2,1024]{3,2,1,0:T(2,128)(2,1)S(1)} copy-done((bf16[8,64,2,1024]{3,2,1,0:T(2,128)(2,1)S(1)}, bf16[8,64,2,1024]{3,2,1,0:T(2,128)(2,1)}, u32[]{:S(2)}) %copy-start) | copy-done | bytes 2097176
  1.6 0.0 copy-start.1
  1.6 0.7 copy-done.1
  2.3 0.0 copy-start.2
  2.3 0.7 copy-done.2
  3.0 82.2 %correlate.1 = bf16[1,2,512,2048]{3,2,1,0:T(8,128)(2,1)S(1)} custom-call(bf16[8,64,2,1024]{3,2,1,0:T(2,128)(2,1)S(1)} %copy-done, s32[1,1024]{1,0:T(1,128)S(1)} %copy-done.2, s32[16,128]{1,0:T(8,128)S(1)} %bitcast.1), custom_call_target="tpu_custom_call" | custom-call | flops 25999998976 | bytes 6291456 | tf_op jit(solution)/shard_map/correlate/pallas_call | solution.py:250
  85.2 2.0 %copy.5 = bf16[1,2,512,2048]{3,2,1,0:T(8,128)(2,1)} copy(bf16[1,2,512,2048]{3,2,1,0:T(8,128)(2,1)S(1)} %correlate.1) | data formatting | bytes 8388608
Async XLA Ops:
  0.0 1.6 %copy-start = (bf16[8,64,2,1024]{3,2,1,0:T(2,128)(2,1)S(1)}, bf16[8,64,2,1024]{3,2,1,0:T(2,128)(2,1)}, u32[]{:S(2)}) copy-start(bf16[8,64,2,1024]{3,2,1,0:T(2,128)(2,1)} %raw.1) | copy-start | bytes 6291460
  1.6 0.7 copy-start.1
  2.3 0.7 copy-start.2

commit v4 on v3

--- a/solution.py
+++ b/solution.py
@@ -12,7 +12,7 @@
 ROWS = 512
 
 
-def kernel(raw, flags, feeds, out, samples, zbuf, obuf, g, onehot, merged, ordered, left, acc, staged,
+def kernel(raw, table, out, samples, zbuf, obuf, g, onehot, merged, ordered, left, acc, staged,
            zs, zr, xs, xr, own_s, own_r, out_s, out_r, fwd_s, fwd_r, core_s, core_r, pair_s, pair_r, write_s):
     fi = lax.axis_index("freq")
     member = lax.axis_index("pair")
@@ -100,8 +100,7 @@
 
     def order(k):
         wait(g.at[k, 1 - core], core_r.at[k])
-        times = pl.ds(pl.multiple_of(k * TC, TC), TC)
-        keep = jnp.broadcast_to((1 - flags[:, times]).astype(jnp.float32), (16, TC)).astype(jnp.bfloat16)
+        keep = jnp.broadcast_to((1 - table[pl.ds(k, 1), :]).astype(jnp.float32), (16, TC)).astype(jnp.bfloat16)
 
         @pl.loop(0, 8)
         def _(b):
@@ -158,7 +157,7 @@
 
     @pl.loop(0, 8)
     def _(b):
-        feed = feeds[pl.ds((b // 4 * 2 + core) * 4 + b % 4, 1), :]
+        feed = table[pl.ds(NC + (b // 4 * 2 + core) * 4 + b % 4, 1), :]
         w, c, l = feed & 7, (feed >> 3) & 1, (feed >> 4) & 1
         xx, zz, h = (feed >> 5) & 3, (feed >> 7) & 7, feed >> 10
         spot = ((((c * 4 + h * 2 + l) * 4 + xx) * 8 + zz) * 8 + w).astype(jnp.float32)
@@ -186,6 +185,10 @@
         def _():
             y_send((s - 1), 0)
 
+        @pl.when((s >= 3) & (s < NC + 3))
+        def _():
+            forward_arrived((s - 3))
+
         @pl.when(s < NC)
         def _():
             x_send(s, 1)
@@ -201,10 +204,6 @@
         @pl.when(s >= 4)
         def _():
             order((s - 4))
-
-        @pl.when((s >= 2) & (s < NC + 2))
-        def _():
-            forward((s - 2))
 
         @pl.when(s >= 4)
         def _():
@@ -220,9 +219,9 @@
             wait(ordered.at[(s - 4), :, 1 - core], pair_r.at[(s - 4)])
             product((s - 4), 1 - core)
 
-        @pl.when((s >= 3) & (s < NC + 3))
-        def _():
-            forward_arrived((s - 3))
+        @pl.when((s >= 1) & (s < NC + 1))
+        def _():
+            forward((s - 1))
 
         return carry
 
@@ -250,7 +249,7 @@
     return pl.pallas_call(
         kernel,
         out_shape=jax.ShapeDtypeStruct((1, 2, ROWS, SLOTS), jnp.bfloat16),
-        in_specs=[vmem, vmem, vmem],
+        in_specs=[vmem, vmem],
         out_specs=pl.BlockSpec(memory_space=pl.ANY),
         scratch_shapes=[
             pltpu.VMEM((NC, 2, 8, 4, 16, TC), jnp.bfloat16),
@@ -272,7 +271,7 @@
         ),
         cost_estimate=pl.CostEstimate(flops=26 * 10**9, bytes_accessed=6 * 2**20, transcendentals=0),
         name="correlate",
-    )(samples, rfi_flags, feed_map.reshape(16, 128))
+    )(samples, jnp.concatenate([rfi_flags.reshape(NC, TC), feed_map.reshape(16, TC)]))
 
 
 def solution(mesh):

time: 87.4 us -> 86.2 us (0.986)
  local copies, waits for them, and re-layouts: 4.99 us -> 3.61 us
    unnamed x7 -> x3, local copies, waits for them, and re-layouts: 4.99 us -> 3.61 us
where the time goes in v4:
time: 86.2 us; the launch traced here: 86 us
  Pallas kernels  81.7 us (95%)
  local copies, waits for them, and re-layouts  3.61 us (4%)
    pallas_call x1, Pallas kernels, local(): pl.pallas_call(kernel, out_shape=jax.ShapeDtypeStruct((1, 2, ROWS, SLOTS)...  81.7 us
    unnamed x3, local copies, waits for them, and re-layouts  3.61 us

profile of v4, /device:TPU:1, one launch (start us, length us, event | category | flops | bytes accessed | tf_op | source)
XLA Modules:
  0.0 86.0 jit_solution(8739853507577589610)
XLA Ops:
  0.0 0.7 pad_add_fusion.table
  0.7 0.0 copy-start
  0.7 1.6 %copy-done = bf16[8,64,2,1024]{3,2,1,0:T(2,128)(2,1)S(1)} copy-done((bf16[8,64,2,1024]{3,2,1,0:T(2,128)(2,1)S(1)}, bf16[8,64,2,1024]{3,2,1,0:T(2,128)(2,1)}, u32[]{:S(2)}) %copy-start) | copy-done | bytes 2097176
  2.3 81.7 %correlate.1 = bf16[1,2,512,2048]{3,2,1,0:T(8,128)(2,1)S(1)} custom-call(bf16[8,64,2,1024]{3,2,1,0:T(2,128)(2,1)S(1)} %copy-done, s32[24,128]{1,0:T(8,128)S(1)} %pad_add_fusion.table), custom_call_target="tpu_custom_call" | custom-call | flops 25999998976 | bytes 6291456 | tf_op jit(solution)/shard_map/correlate/pallas_call | solution.py:249
  84.0 2.0 %copy.5 = bf16[1,2,512,2048]{3,2,1,0:T(8,128)(2,1)} copy(bf16[1,2,512,2048]{3,2,1,0:T(8,128)(2,1)S(1)} %correlate.1) | data formatting | bytes 8388608
Async XLA Ops:
  0.7 1.6 %copy-start = (bf16[8,64,2,1024]{3,2,1,0:T(2,128)(2,1)S(1)}, bf16[8,64,2,1024]{3,2,1,0:T(2,128)(2,1)}, u32[]{:S(2)}) copy-start(bf16[8,64,2,1024]{3,2,1,0:T(2,128)(2,1)} %raw.1) | copy-start | bytes 6291460
